TPU v7x, 256 devices: a whole 4x4x8 slice. The times are simulated.
256 devices in a mesh: section: 4 (over x_hi, core), ctx: 64 (over x_lo, y, z).
Axes of the slice: x: 4 (x_hi: 2, x_lo: 2; x = x_hi * 2 + x_lo), y: 4, z: 8, core: 2. Of those that a mesh axis runs over, the one named last changes fastest.
Arguments:
- grad_next: bfloat16 [4, 8192, 4096], P('section', 'ctx'), may hold values from -0.0625 to 0.0625
- gate: bfloat16 [4, 8192, 4096], P('section', 'ctx'), may hold values from -6 to 6
- conv_input: bfloat16 [4, 8192, 4096], P('section', 'ctx'), may hold values from -6 to 6
- saved_conv: bfloat16 [4, 8192, 4096], P('section', 'ctx'), may hold values from -320 to 320
- long_filter: bfloat16 [4, 8192, 4096], P('section', 'ctx'), may hold values from -16 to 16
Outputs:
- grad_input: bfloat16 [4, 8192, 4096], P('section', 'ctx')
- grad_gate: bfloat16 [4, 8192, 4096], P('section', 'ctx')
- filter_grad: bfloat16 [4, 8192, 4096], P('section', 'ctx')
All inputs are finite; a program needn't handle non-finite values.
Results may differ from a plain program's by a relative error of at most 0.0095.
Values may be sent and summed in bfloat16 or wider, within the bound.
A program may use at most 192 MiB of HBM per device.

v0:
```python
import math

import jax
import jax.numpy as jnp
from jax import lax
from jax.sharding import PartitionSpec as P


def passed_along(shard, axis, by):
    size = lax.axis_size(axis)
    return lax.ppermute(shard, axis, [(i, (i + by) % size) for i in range(size)])


def outer_tables(ctx_count):
    outer_len = 2 * ctx_count
    outer_idx = jnp.arange(outer_len, dtype=jnp.int32)
    positions = jnp.arange(ctx_count, dtype=jnp.int32)
    angle_outer = (
        2.0
        * math.pi
        / outer_len
        * (outer_idx[:, None] * positions[None, :] % outer_len).astype(jnp.float32)
    )
    return (jnp.cos(angle_outer).astype(jnp.bfloat16), (-jnp.sin(angle_outer)).astype(jnp.bfloat16))


def twisted_rows(rows_k1, block_len, outer_len):
    full_len = outer_len * block_len
    inner_idx = jnp.arange(block_len, dtype=jnp.int32)
    freq = rows_k1[:, None, None] + outer_len * inner_idx[None, :, None]
    angle = (
        2.0 * math.pi / full_len * (inner_idx[None, None, :] * freq % full_len).astype(jnp.float32)
    )
    return (jnp.cos(angle).astype(jnp.bfloat16), (-jnp.sin(angle)).astype(jnp.bfloat16))


def forward_matrix(tw_re, tw_im):
    top = jnp.stack([tw_re, -tw_im], axis=2)
    low = jnp.stack([tw_im, tw_re], axis=2)
    return jnp.stack([top, low], axis=1)


def inverse_matrix(tw_re, tw_im):
    flip_re = tw_re.transpose(0, 2, 1)
    flip_im = tw_im.transpose(0, 2, 1)
    top = jnp.stack([flip_re, flip_im], axis=2)
    low = jnp.stack([-flip_im, flip_re], axis=2)
    return jnp.stack([top, low], axis=1)


def to_blocks(signal):
    return lax.all_to_all(signal, "ctx", split_axis=1, concat_axis=0, tiled=True)


def from_blocks(signal):
    return lax.all_to_all(signal, "ctx", split_axis=0, concat_axis=1, tiled=True)


def first_pass(blocks, cos_outer, sin_outer):
    ctx_count, local_rows, channels = blocks.shape
    outer_len = cos_outer.shape[0]
    matrix = jnp.stack([cos_outer, sin_outer], axis=1).reshape(2 * outer_len, ctx_count)
    mixed_out = jnp.dot(
        matrix, blocks.reshape(ctx_count, local_rows * channels), preferred_element_type=jnp.float32
    )
    return mixed_out.astype(jnp.bfloat16).reshape(outer_len, 2, local_rows, channels)


def second_pass(row_data, matrix):
    return jnp.einsum("koqij,kijw->koqw", matrix, row_data, preferred_element_type=jnp.float32)


def third_pass(spectrum, matrix):
    return jnp.einsum(
        "kojiq,kiqw->kojw", matrix, spectrum, preferred_element_type=jnp.float32
    ).astype(jnp.bfloat16)


def fourth_pass(row_data, cos_outer, sin_outer, inv_scale):
    outer_len = row_data.shape[0]
    local_rows = row_data.shape[2]
    channels = row_data.shape[3]
    matrix = jnp.stack([cos_outer, sin_outer], axis=1).reshape(2 * outer_len, -1).T
    summed = jnp.dot(
        matrix,
        row_data.reshape(2 * outer_len, local_rows * channels),
        preferred_element_type=jnp.float32,
    )
    return (summed * inv_scale).reshape(-1, local_rows, channels).astype(jnp.bfloat16)


def cross_conj(left_spec, right_spec):
    cross_re = left_spec[:, 0] * right_spec[:, 0] + left_spec[:, 1] * right_spec[:, 1]
    cross_im = left_spec[:, 1] * right_spec[:, 0] - left_spec[:, 0] * right_spec[:, 1]
    return jnp.stack([cross_re, cross_im], axis=1).astype(jnp.bfloat16)


def spectrum_split(signal, cos_outer, sin_outer, fwd_matrix):
    block_len, channels = signal.shape
    blocks = to_blocks(signal.reshape(1, block_len, channels))
    firsts = first_pass(blocks, cos_outer, sin_outer)
    return second_pass(
        lax.all_to_all(firsts, "ctx", split_axis=0, concat_axis=2, tiled=True), matrix=fwd_matrix
    )


def signal_split(spectrum, cos_outer, sin_outer, inv_matrix, inv_scale):
    turned = third_pass(spectrum, inv_matrix)
    blocks = fourth_pass(
        lax.all_to_all(turned, "ctx", split_axis=2, concat_axis=0, tiled=True),
        cos_outer=cos_outer,
        sin_outer=sin_outer,
        inv_scale=inv_scale,
    )
    return from_blocks(blocks)[0]


def per_device(grad_next, gate, conv_input, saved_conv, long_filter):
    ctx_count = lax.axis_size("ctx")
    my_index = lax.axis_index("ctx")
    block_len = gate.shape[1]
    outer_len = 2 * ctx_count
    cos_outer, sin_outer = outer_tables(ctx_count)
    inv_scale = 1.0 / (outer_len * block_len)
    grad_out = passed_along(grad_next, "section", -1)[0]
    grad_gate = (grad_out.astype(jnp.float32) * saved_conv[0].astype(jnp.float32)).astype(
        jnp.bfloat16
    )
    grad_conv = (grad_out.astype(jnp.float32) * gate[0].astype(jnp.float32)).astype(jnp.bfloat16)
    local_k1 = outer_len // ctx_count
    rows_k1 = my_index * local_k1 + jnp.arange(local_k1, dtype=jnp.int32)
    tw_re, tw_im = twisted_rows(rows_k1, block_len, outer_len)
    fwd_matrix = forward_matrix(tw_re, tw_im)
    inv_matrix = inverse_matrix(tw_re, tw_im)
    spec_input = spectrum_split(conv_input[0], cos_outer, sin_outer, fwd_matrix)
    spec_grad = spectrum_split(grad_conv, cos_outer, sin_outer, fwd_matrix)
    spec_filter = spectrum_split(long_filter[0], cos_outer, sin_outer, fwd_matrix)
    grad_input = signal_split(
        cross_conj(spec_grad, spec_filter), cos_outer, sin_outer, inv_matrix, inv_scale
    )
    filter_grad = signal_split(
        cross_conj(spec_grad, spec_input), cos_outer, sin_outer, inv_matrix, inv_scale
    )
    return (grad_input[None], grad_gate[None], filter_grad[None])


def solution(mesh):
    in_specs = (
        P("section", "ctx", None),
        P("section", "ctx", None),
        P("section", "ctx", None),
        P("section", "ctx", None),
        P("section", "ctx", None),
    )
    out_specs = (P("section", "ctx", None), P("section", "ctx", None), P("section", "ctx", None))
    return jax.shard_map(
        per_device, mesh=mesh, in_specs=in_specs, out_specs=out_specs, check_vma=False
    )
```

profile of v0, /device:TPU:2, one launch (start us, length us, event | category | flops | bytes accessed | tf_op | source)
XLA Modules:
  0.0 728.1 jit_solution(496568881710132713)
XLA Ops:
  0.6 3.6 copy.120
  4.8 7.1 reduce.8
  11.9 1.5 reshape.329
  13.4 13.2 %all-to-all-start.2 = ((bf16[64,2,4096]{2,1,0:T(2,128)(2,1)}), bf16[64,2,4096]{2,1,0:T(2,128)(2,1)S(1)}, u32[]{:S(2)}, u32[]{:S(2)}) async-start(bf16[64,2,4096]{2,1,0:T(2,128)(2,1)} %reshape.329), calls=%async_computation.2 | async-start | bytes 2097152 | tf_op jit(solution)/shard_map/all_to_all | solution.py:52
  26.6 1.3 collective-permute-start
  27.9 3.6 copy.119
  31.5 8.0 %reduce.6 = bf16[128,4096]{1,0:T(8,128)(2,1)} reduce(bf16[128,1,4096]{2,1,0:T(2,128)(2,1)S(1)} %bitcast.101, bf16[]{:T(256)} %broadcast.367), dimensions={1}, to_apply=%bitcast.89.reduce_sub_computation | reduce | bytes 2097154
  39.6 2.7 reshape.333
  42.2 14.0 %all-to-all-done.2 = bf16[64,2,4096]{2,1,0:T(2,128)(2,1)S(1)} async-done(((bf16[64,2,4096]{2,1,0:T(2,128)(2,1)}), bf16[64,2,4096]{2,1,0:T(2,128)(2,1)S(1)}, u32[]{:S(2)}, u32[]{:S(2)}) %all-to-all-start.2) | async-done | bytes 1048608 | tf_op jit(solution)/shard_map/all_to_all | solution.py:52
  57.2 5.9 all-to-all-start.6
  63.1 2.7 fusion.10
  65.8 2.4 copy.121
  68.2 8.0 %reduce.7 = bf16[128,4096]{1,0:T(8,128)(2,1)} reduce(bf16[128,1,4096]{2,1,0:T(2,128)(2,1)S(1)} %bitcast.100, bf16[]{:T(256)} %broadcast.367), dimensions={1}, to_apply=%bitcast.91.reduce_sub_computation | reduce | bytes 2097154
  76.2 2.6 reshape.331
  78.8 12.9 %all-to-all-done.6 = bf16[64,2,4096]{2,1,0:T(2,128)(2,1)S(1)} async-done(((bf16[64,2,4096]{2,1,0:T(2,128)(2,1)}), bf16[64,2,4096]{2,1,0:T(2,128)(2,1)S(1)}, u32[]{:S(2)}, u32[]{:S(2)}) %all-to-all-start.6) | async-done | bytes 1048608 | tf_op jit(solution)/shard_map/all_to_all | solution.py:52
  91.7 5.9 all-to-all-start
  97.8 6.5 reshape.330
  104.3 7.2 bitcast_reduce_fusion.2
  111.5 1.5 reshape.307
  113.0 3.2 convolution_convert_fusion.1
  116.2 7.8 %reshape.308 = bf16[128,2,2,4096]{3,2,1,0:T(2,128)(2,1)} reshape(bf16[256,8192]{1,0:T(8,128)(2,1)} %convolution_convert_fusion.1) | data formatting | bytes 8388608 | tf_op jit(solution)/shard_map/reshape | solution.py:66
  125.1 10.8 %all-to-all-start.3 = ((bf16[128,2,2,4096]{3,2,1,0:T(2,128)(2,1)}), bf16[128,2,2,4096]{3,2,1,0:T(2,128)(2,1)}, u32[]{:S(2)}, u32[]{:S(2)}) async-start(bf16[128,2,2,4096]{3,2,1,0:T(2,128)(2,1)} %reshape.308), calls=%async_computation.3 | async-start | bytes 8388608 | tf_op jit(solution)/shard_map/all_to_all | solution.py:103
  137.0 6.2 bitcast_reduce_fusion
  143.7 3.2 convolution_convert_fusion
  146.8 7.8 %reshape.311 = bf16[128,2,2,4096]{3,2,1,0:T(2,128)(2,1)} reshape(bf16[256,8192]{1,0:T(8,128)(2,1)} %convolution_convert_fusion) | data formatting | bytes 8388608 | tf_op jit(solution)/shard_map/reshape | solution.py:66
  154.6 73.6 %all-to-all-done.3 = bf16[128,2,2,4096]{3,2,1,0:T(2,128)(2,1)} async-done(((bf16[128,2,2,4096]{3,2,1,0:T(2,128)(2,1)}), bf16[128,2,2,4096]{3,2,1,0:T(2,128)(2,1)}, u32[]{:S(2)}, u32[]{:S(2)}) %all-to-all-start.3) | async-done | bytes 4194336 | tf_op jit(solution)/shard_map/all_to_all | solution.py:103
  228.3 8.2 %all-to-all-start.7 = ((bf16[128,2,2,4096]{3,2,1,0:T(2,128)(2,1)}), bf16[128,2,2,4096]{3,2,1,0:T(2,128)(2,1)}, u32[]{:S(2)}, u32[]{:S(2)}) async-start(bf16[128,2,2,4096]{3,2,1,0:T(2,128)(2,1)} %reshape.311), calls=%async_computation.7 | async-start | bytes 8388608 | tf_op jit(solution)/shard_map/all_to_all | solution.py:103
  236.5 6.5 reshape.332
  243.0 6.2 bitcast_reduce_fusion.1
  249.6 3.2 convolution_convert_fusion.2
  252.8 7.8 %reshape.306 = bf16[128,2,2,4096]{3,2,1,0:T(2,128)(2,1)} reshape(bf16[256,8192]{1,0:T(8,128)(2,1)} %convolution_convert_fusion.2) | data formatting | bytes 8388608 | tf_op jit(solution)/shard_map/reshape | solution.py:66
  260.6 67.6 %all-to-all-done.7 = bf16[128,2,2,4096]{3,2,1,0:T(2,128)(2,1)} async-done(((bf16[128,2,2,4096]{3,2,1,0:T(2,128)(2,1)}), bf16[128,2,2,4096]{3,2,1,0:T(2,128)(2,1)}, u32[]{:S(2)}, u32[]{:S(2)}) %all-to-all-start.7) | async-done | bytes 4194336 | tf_op jit(solution)/shard_map/all_to_all | solution.py:103
  328.2 7.8 %all-to-all-start.1 = ((bf16[128,2,2,4096]{3,2,1,0:T(2,128)(2,1)}), bf16[128,2,2,4096]{3,2,1,0:T(2,128)(2,1)}, u32[]{:S(2)}, u32[]{:S(2)}) async-start(bf16[128,2,2,4096]{3,2,1,0:T(2,128)(2,1)} %reshape.306), calls=%async_computation.1 | async-start | bytes 8388608 | tf_op jit(solution)/shard_map/all_to_all | solution.py:103
  338.3 9.9 %copy.117 = bf16[64,2,2,2,4096]{4,3,0,2,1:T(2,128)(2,1)} copy(bf16[64,2,2,2,4096]{4,3,2,1,0:T(2,128)(2,1)} %bitcast.11) | data formatting | bytes 8388608 | tf_op jit(solution)/shard_map/all_to_all | solution.py:103
  348.3 7.2 reshape.315
  355.4 9.9 %copy.116 = bf16[64,2,2,2,4096]{4,3,0,2,1:T(2,128)(2,1)} copy(bf16[64,2,2,2,4096]{4,3,2,1,0:T(2,128)(2,1)} %bitcast.22) | data formatting | bytes 8388608 | tf_op jit(solution)/shard_map/all_to_all | solution.py:103
  365.4 7.4 %reshape.319 = bf16[2,2,128,4096,1]{3,2,1,0,4:T(8,128)(2,1)} reshape(bf16[2,2,64,2,4096]{4,3,2,1,0:T(2,128)(2,1)} %bitcast.94) | data formatting | bytes 8388608 | tf_op jit(solution)/shard_map/all_to_all | solution.py:103
  372.8 6.8 convolution_bitcast_fusion.1
  379.6 4.5 convolution_bitcast_fusion
  384.1 43.1 %all-to-all-done.1 = bf16[128,2,2,4096]{3,2,1,0:T(2,128)(2,1)} async-done(((bf16[128,2,2,4096]{3,2,1,0:T(2,128)(2,1)}), bf16[128,2,2,4096]{3,2,1,0:T(2,128)(2,1)}, u32[]{:S(2)}, u32[]{:S(2)}) %all-to-all-start.1) | async-done | bytes 4194336 | tf_op jit(solution)/shard_map/all_to_all | solution.py:103
  427.2 9.9 %copy.118 = bf16[64,2,2,2,4096]{4,3,0,2,1:T(2,128)(2,1)} copy(bf16[64,2,2,2,4096]{4,3,2,1,0:T(2,128)(2,1)} %bitcast.6) | data formatting | bytes 8388608 | tf_op jit(solution)/shard_map/all_to_all | solution.py:103
  437.1 7.2 reshape.313
  444.4 3.4 convolution_bitcast_fusion.2
  447.8 8.8 %add_convert_fusion = (bf16[2,1,128,4096]{3,2,1,0:T(8,128)(2,1)S(1)}, bf16[2,1,128,4096]{3,2,1,0:T(8,128)(2,1)S(1)}, bf16[2,1,128,4096]{3,2,1,0:T(8,128)(2,1)S(1)}, bf16[2,1,128,4096]{3,2,1,0:T(8,128)(2,1)}) fusion(f32[2,2,128,4096]{3,2,1,0:T(8,128)} %convolution_bitcast_fusion, f32[2,2,128,4096]{3,2,1,0:T(8,128)S(1)} %convolution_bitcast_fusion.2, ...), kind=kLoop, calls=%fused_computation.25 | loop fusion | flops 16777216 | bytes 33554432 | tf_op jit(solution)/shard_map/convert
  456.7 1.3 bitcast_convert_fusion
  457.9 6.3 copy.92
  464.3 7.8 %all-to-all-start.8 = ((bf16[2,2,128,4096]{3,1,0,2:T(2,128)(2,1)}), bf16[2,2,128,4096]{3,1,0,2:T(2,128)(2,1)}, u32[]{:S(2)}, u32[]{:S(2)}) async-start(bf16[2,2,128,4096]{3,1,0,2:T(2,128)(2,1)} %copy.92), calls=%async_computation.8 | async-start | bytes 8388608 | tf_op jit(solution)/shard_map/all_to_all | solution.py:110
  472.1 2.9 bitcast_convert_fusion.1
  475.0 6.3 copy.87
  481.3 82.0 %all-to-all-done.8 = bf16[2,2,128,4096]{3,1,0,2:T(2,128)(2,1)} async-done(((bf16[2,2,128,4096]{3,1,0,2:T(2,128)(2,1)}), bf16[2,2,128,4096]{3,1,0,2:T(2,128)(2,1)}, u32[]{:S(2)}, u32[]{:S(2)}) %all-to-all-start.8) | async-done | bytes 4194336 | tf_op jit(solution)/shard_map/all_to_all | solution.py:110
  563.3 8.1 %all-to-all-start.4 = ((bf16[2,2,128,4096]{3,1,0,2:T(2,128)(2,1)}), bf16[2,2,128,4096]{3,1,0,2:T(2,128)(2,1)}, u32[]{:S(2)}, u32[]{:S(2)}) async-start(bf16[2,2,128,4096]{3,1,0,2:T(2,128)(2,1)} %copy.87), calls=%async_computation.4 | async-start | bytes 8388608 | tf_op jit(solution)/shard_map/all_to_all | solution.py:110
  571.4 10.6 %copy.93 = bf16[2,2,64,2,4096]{4,3,1,0,2:T(2,128)(2,1)S(1)} copy(bf16[2,2,64,2,4096]{4,1,0,3,2:T(2,128)(2,1)} %bitcast.31) | data formatting | bytes 8388608 | tf_op jit(solution)/shard_map/all_to_all | solution.py:110
  582.1 4.7 copy.105
  587.6 1.6 convert_element_type.194
  589.2 73.1 %all-to-all-done.4 = bf16[2,2,128,4096]{3,1,0,2:T(2,128)(2,1)} async-done(((bf16[2,2,128,4096]{3,1,0,2:T(2,128)(2,1)}), bf16[2,2,128,4096]{3,1,0,2:T(2,128)(2,1)}, u32[]{:S(2)}, u32[]{:S(2)}) %all-to-all-start.4) | async-done | bytes 4194336 | tf_op jit(solution)/shard_map/all_to_all | solution.py:110
  662.3 7.7 %all-to-all-start.9 = ((bf16[64,2,4096]{2,1,0:T(2,128)(2,1)}), bf16[64,2,4096]{2,1,0:T(2,128)(2,1)S(1)}, u32[]{:S(2)}, u32[]{:S(2)}) async-start(bf16[64,2,4096]{2,1,0:T(2,128)(2,1)} %convert_element_type.194), calls=%async_computation.9 | async-start | bytes 2097152 | tf_op jit(solution)/shard_map/all_to_all | solution.py:56
  670.0 10.6 %copy.88 = bf16[2,2,64,2,4096]{4,3,1,0,2:T(2,128)(2,1)S(1)} copy(bf16[2,2,64,2,4096]{4,1,0,3,2:T(2,128)(2,1)} %bitcast.20) | data formatting | bytes 8388608 | tf_op jit(solution)/shard_map/all_to_all | solution.py:110
  680.7 4.7 copy.104
  686.3 1.6 convert_element_type.188
  687.9 8.0 %all-to-all-done.9 = bf16[64,2,4096]{2,1,0:T(2,128)(2,1)S(1)} async-done(((bf16[64,2,4096]{2,1,0:T(2,128)(2,1)}), bf16[64,2,4096]{2,1,0:T(2,128)(2,1)S(1)}, u32[]{:S(2)}, u32[]{:S(2)}) %all-to-all-start.9) | async-done | bytes 1048608 | tf_op jit(solution)/shard_map/all_to_all | solution.py:56
  695.8 5.3 all-to-all-start.5
  701.2 1.2 all_to_all.124
  702.4 24.1 %all-to-all-done.5 = bf16[64,2,4096]{2,1,0:T(2,128)(2,1)S(1)} async-done(((bf16[64,2,4096]{2,1,0:T(2,128)(2,1)}), bf16[64,2,4096]{2,1,0:T(2,128)(2,1)S(1)}, u32[]{:S(2)}, u32[]{:S(2)}) %all-to-all-start.5) | async-done | bytes 1048608 | tf_op jit(solution)/shard_map/all_to_all | solution.py:56
  726.5 1.2 all_to_all.114
  (26 shorter events, 9.0 us)
Async XLA Ops:
  13.4 42.8 %all-to-all-start.2 = ((bf16[64,2,4096]{2,1,0:T(2,128)(2,1)}), bf16[64,2,4096]{2,1,0:T(2,128)(2,1)S(1)}, u32[]{:S(2)}, u32[]{:S(2)}) async-start(bf16[64,2,4096]{2,1,0:T(2,128)(2,1)} %reshape.329), calls=%async_computation.2 | async-start | bytes 2097152 | tf_op jit(solution)/shard_map/all_to_all | solution.py:52
  26.6 36.5 %collective-permute-start = (bf16[1,128,4096]{2,1,0:T(8,128)(2,1)}, bf16[1,128,4096]{2,1,0:T(8,128)(2,1)}, u32[]{:S(2)}, u32[]{:S(2)}) collective-permute-start(bf16[1,128,4096]{2,1,0:T(8,128)(2,1)} %param.5), channel_id=1, source_target_pairs={{0,192},{64,0},{128,64},{192,128},{1,193},{65,1},{129,65},{193,129... | collective-permute-start | bytes 3145736 | tf_op jit(solution)/shard_map/ppermute | solution.py:11
  39.6 23.5 %copy-start.2 = (bf16[1,128,4096]{2,1,0:T(8,128)(2,1)S(1)}, bf16[1,128,4096]{2,1,0:T(8,128)(2,1)}, u32[]{:S(2)}) copy-start(bf16[1,128,4096]{2,1,0:T(8,128)(2,1)} %param.8) | copy-start | bytes 3145732
  39.6 23.5 %copy-start.3 = (bf16[1,128,4096]{2,1,0:T(8,128)(2,1)S(1)}, bf16[1,128,4096]{2,1,0:T(8,128)(2,1)}, u32[]{:S(2)}) copy-start(bf16[1,128,4096]{2,1,0:T(8,128)(2,1)} %param.6) | copy-start | bytes 3145732
  56.2 1.0 copy-start.1
  57.2 34.5 %all-to-all-start.6 = ((bf16[64,2,4096]{2,1,0:T(2,128)(2,1)}), bf16[64,2,4096]{2,1,0:T(2,128)(2,1)S(1)}, u32[]{:S(2)}, u32[]{:S(2)}) async-start(bf16[64,2,4096]{2,1,0:T(2,128)(2,1)} %reshape.333), calls=%async_computation.6 | async-start | bytes 2097152 | tf_op jit(solution)/shard_map/all_to_all | solution.py:52
  91.7 33.5 %all-to-all-start = ((bf16[64,2,4096]{2,1,0:T(2,128)(2,1)}), bf16[64,2,4096]{2,1,0:T(2,128)(2,1)}, u32[]{:S(2)}, u32[]{:S(2)}) async-start(bf16[64,2,4096]{2,1,0:T(2,128)(2,1)} %reshape.331), calls=%async_computation | async-start | bytes 2097152 | tf_op jit(solution)/shard_map/all_to_all | solution.py:52
  125.1 103.1 %all-to-all-start.3 = ((bf16[128,2,2,4096]{3,2,1,0:T(2,128)(2,1)}), bf16[128,2,2,4096]{3,2,1,0:T(2,128)(2,1)}, u32[]{:S(2)}, u32[]{:S(2)}) async-start(bf16[128,2,2,4096]{3,2,1,0:T(2,128)(2,1)} %reshape.308), calls=%async_computation.3 | async-start | bytes 8388608 | tf_op jit(solution)/shard_map/all_to_all | solution.py:103
  228.3 99.9 %all-to-all-start.7 = ((bf16[128,2,2,4096]{3,2,1,0:T(2,128)(2,1)}), bf16[128,2,2,4096]{3,2,1,0:T(2,128)(2,1)}, u32[]{:S(2)}, u32[]{:S(2)}) async-start(bf16[128,2,2,4096]{3,2,1,0:T(2,128)(2,1)} %reshape.311), calls=%async_computation.7 | async-start | bytes 8388608 | tf_op jit(solution)/shard_map/all_to_all | solution.py:103
  328.2 99.1 %all-to-all-start.1 = ((bf16[128,2,2,4096]{3,2,1,0:T(2,128)(2,1)}), bf16[128,2,2,4096]{3,2,1,0:T(2,128)(2,1)}, u32[]{:S(2)}, u32[]{:S(2)}) async-start(bf16[128,2,2,4096]{3,2,1,0:T(2,128)(2,1)} %reshape.306), calls=%async_computation.1 | async-start | bytes 8388608 | tf_op jit(solution)/shard_map/all_to_all | solution.py:103
  372.8 6.8 copy-start
  464.3 99.0 %all-to-all-start.8 = ((bf16[2,2,128,4096]{3,1,0,2:T(2,128)(2,1)}), bf16[2,2,128,4096]{3,1,0,2:T(2,128)(2,1)}, u32[]{:S(2)}, u32[]{:S(2)}) async-start(bf16[2,2,128,4096]{3,1,0,2:T(2,128)(2,1)} %copy.92), calls=%async_computation.8 | async-start | bytes 8388608 | tf_op jit(solution)/shard_map/all_to_all | solution.py:110
  563.3 99.0 %all-to-all-start.4 = ((bf16[2,2,128,4096]{3,1,0,2:T(2,128)(2,1)}), bf16[2,2,128,4096]{3,1,0,2:T(2,128)(2,1)}, u32[]{:S(2)}, u32[]{:S(2)}) async-start(bf16[2,2,128,4096]{3,1,0,2:T(2,128)(2,1)} %copy.87), calls=%async_computation.4 | async-start | bytes 8388608 | tf_op jit(solution)/shard_map/all_to_all | solution.py:110
  662.3 33.5 %all-to-all-start.9 = ((bf16[64,2,4096]{2,1,0:T(2,128)(2,1)}), bf16[64,2,4096]{2,1,0:T(2,128)(2,1)S(1)}, u32[]{:S(2)}, u32[]{:S(2)}) async-start(bf16[64,2,4096]{2,1,0:T(2,128)(2,1)} %convert_element_type.194), calls=%async_computation.9 | async-start | bytes 2097152 | tf_op jit(solution)/shard_map/all_to_all | solution.py:56
  695.8 30.6 %all-to-all-start.5 = ((bf16[64,2,4096]{2,1,0:T(2,128)(2,1)}), bf16[64,2,4096]{2,1,0:T(2,128)(2,1)S(1)}, u32[]{:S(2)}, u32[]{:S(2)}) async-start(bf16[64,2,4096]{2,1,0:T(2,128)(2,1)} %convert_element_type.188), calls=%async_computation.5 | async-start | bytes 2097152 | tf_op jit(solution)/shard_map/all_to_all | solution.py:56
where the time goes:
time: 738 us; the launch traced here: 728 us
  waiting for transfers between devices  399 us (54%)
  local copies, waits for them, and re-layouts  178 us (24%)
  starting transfers between devices  82 us (11%)
  other arithmetic  37.1 us (5%)
  matrix products  30.2 us (4%)
    all_to_all x3, waiting for transfers between devices, spectrum_split(): lax.all_to_all(firsts, 'ctx', split_axis=0, concat_axis=2, tiled=True)  184 us
    all_to_all x2, waiting for transfers between devices, signal_split(): lax.all_to_all(turned, 'ctx', split_axis=2, concat_axis=0, tiled=True)  155 us
    all_to_all x6, local copies, waits for them, and re-layouts, spectrum_split(): lax.all_to_all(firsts, 'ctx', split_axis=0, concat_axis=2, tiled=True)  51.6 us
    unnamed x19, local copies, waits for them, and re-layouts  39 us
    all_to_all x2, waiting for transfers between devices, from_blocks(): lax.all_to_all(signal, 'ctx', split_axis=0, concat_axis=1, tiled=True)  32 us
    all_to_all x3, waiting for transfers between devices, to_blocks(): lax.all_to_all(signal, 'ctx', split_axis=1, concat_axis=0, tiled=True)  28 us
    all_to_all x3, starting transfers between devices, spectrum_split(): lax.all_to_all(firsts, 'ctx', split_axis=0, concat_axis=2, tiled=True)  26.8 us
    all_to_all x3, starting transfers between devices, to_blocks(): lax.all_to_all(signal, 'ctx', split_axis=1, concat_axis=0, tiled=True)  25 us
  transfers between devices with their start and end apart: 11, of which 10 were waited for; matrix products, arithmetic and copies ran while one was open for 26% of the time, Pallas kernels for 0%

commit v1 on v0

v1 whole, which is shorter than its diff:
```python
import functools
import math

import jax
import jax.numpy as jnp
import numpy as np
from jax import lax
from jax.experimental import pallas as pl
from jax.experimental.pallas import tpu as pltpu
from jax.sharding import PartitionSpec as P

MESH = pl.DeviceIdType.MESH
BF16 = jnp.bfloat16
F32 = jnp.float32

N_CTX = 64
BLOCK = 128
CHANNELS = 4096
HALF = CHANNELS // 2
WIDTH = HALF // N_CTX
OUTER = 2 * N_CTX
FULL = OUTER * BLOCK
SLOTS = N_CTX


def tables():
    k1 = np.arange(N_CTX + 1, dtype=np.int32)
    at = np.arange(N_CTX, dtype=np.int32)
    step = np.float32(2.0 * math.pi / OUTER)
    angle = step * ((k1[:, None] * at[None, :]) % OUTER).astype(np.float32)
    cos = np.cos(angle).astype(jnp.bfloat16).astype(np.float32)
    sin = (-np.sin(angle)).astype(jnp.bfloat16).astype(np.float32)
    rows = np.stack([cos[:N_CTX], sin[:N_CTX]], axis=1)
    rows[0, 1] = cos[N_CTX]
    weight = np.full((SLOTS, 2, 1), 2.0 / FULL, np.float32)
    weight[0] = 1.0 / FULL
    eye = np.eye(8, dtype=np.float32)
    outer_fwd = np.kron(rows.reshape(2 * SLOTS, N_CTX), eye)
    outer_inv = np.kron((rows * weight).reshape(2 * SLOTS, N_CTX).T, eye)
    j = np.arange(BLOCK, dtype=np.int32)
    freq = k1[:, None, None] + OUTER * j[None, :, None]
    step = np.float32(2.0 * math.pi / FULL)
    angle = step * ((j[None, None, :] * freq) % FULL).astype(np.float32)
    re, im = np.cos(angle), -np.sin(angle)
    top = np.concatenate([re, -im], axis=2)
    low = np.concatenate([im, re], axis=2)
    twist = np.concatenate([top, low], axis=1)
    twist[0, :, BLOCK:] = 0.0
    twist[N_CTX] = np.concatenate([np.zeros((2 * BLOCK, BLOCK)), np.concatenate([re[N_CTX], im[N_CTX]], axis=0)], axis=1)
    turn = twist.transpose(0, 2, 1)
    return [t.astype(jnp.bfloat16) for t in (outer_fwd, outer_inv, twist, turn)]


def lane_group(shape):
    return lax.broadcasted_iota(jnp.int32, shape, len(shape) - 1) // WIDTH


def pick(groups, parts):
    out = parts[3]
    for g in (2, 1, 0):
        out = jnp.where(groups == g, parts[g], out)
    return out


def rolled(value, shift):
    return value if isinstance(shift, int) and shift % 128 == 0 else pltpu.roll(value, shift % 128 if isinstance(shift, int) else shift, 1)


def pack_signal(src, dst, half, row):
    groups = lane_group((32, 128))

    def body(e, carry):
        cols = pl.ds(pl.multiple_of(half * HALF + e * 128, 128), 128)
        quarters = [src[32 * q : 32 * q + 32, cols].astype(F32) for q in range(4)]
        for g in range(4):
            parts = [rolled(quarters[q], 32 * (q - g)) for q in range(4)]
            dst[4 * e + g, row : row + 32, :] = pick(groups, parts).astype(BF16)
        return carry

    lax.fori_loop(0, 16, body, 0)


def unpack_outputs(src, filter_out, input_out, half):
    groups = lane_group((64, 128))

    def body(e, carry):
        cols = pl.ds(pl.multiple_of(half * HALF + e * 128, 128), 128)
        got = [src[4 * e + g].astype(F32) for g in range(4)]
        for at in range(4):
            parts = [rolled(got[g], 32 * (g - at)) for g in range(4)]
            value = pick(groups, parts).astype(BF16)
            out = (filter_out, input_out)[at % 2]
            out[64 * (at // 2) : 64 * (at // 2) + 64, cols] = value
        return carry

    lax.fori_loop(0, 16, body, 0)


def first_pass(both, grad, outer_fwd, firsts):
    groups = lane_group((N_CTX * 16, 128))

    def body(jb, carry):
        q = jb // 2
        row = pl.multiple_of((jb % 2) * 16, 16)
        take = lambda ref, at: ref[:, pl.ds(at, 16), :].astype(F32).reshape(N_CTX * 16, 128)
        x_in, x_fi, x_gr = take(both, row), take(both, row + 32), take(grad, row)
        shift = 128 - 32 * q
        parts = [
            pltpu.roll(x_in, shift % 128, 1),
            pltpu.roll(x_fi, (shift + 32) % 128, 1),
            pltpu.roll(x_gr, (shift + 64) % 128, 1),
            pltpu.roll(x_gr, (shift + 96) % 128, 1),
        ]
        x = pick(groups, parts).reshape(N_CTX, 16, 128)
        x = jnp.concatenate(
            [x[:, 8 * h : 8 * h + 8].reshape(N_CTX * 8, 128).astype(BF16) for h in range(2)], axis=1
        )
        for mb in range(2):
            y = jnp.dot(outer_fwd[512 * mb : 512 * mb + 512, :], x, preferred_element_type=F32)
            y = jnp.concatenate([y[:, 128 * h : 128 * h + 128].reshape(64, 8, 128) for h in range(2)], axis=1)
            firsts[64 * mb : 64 * mb + 64, pl.ds(pl.multiple_of(jb * 16, 16), 16), :] = y.astype(BF16)
        return carry

    lax.fori_loop(0, 8, body, 0)


def middle_passes(firsts, twist, turn, turned):
    low = lax.broadcasted_iota(jnp.int32, (64, 128), 1) < 64

    def one(k1, slot):
        data = firsts[pl.ds(2 * slot, 2)].reshape(2 * BLOCK, 128)
        spec = jnp.dot(twist[k1], data, preferred_element_type=F32)
        re, im = spec[:BLOCK], spec[BLOCK:]
        grad_re, grad_im = pltpu.roll(re, 64, 1), pltpu.roll(im, 64, 1)
        cross = jnp.concatenate(
            [(grad_re * re + grad_im * im).astype(BF16), (grad_im * re - grad_re * im).astype(BF16)], axis=0
        )
        return jnp.dot(turn[k1], cross, preferred_element_type=F32)

    def keep(slot, value):
        for part in range(2):
            at = part * BLOCK
            both = jnp.where(low, value[at : at + 64], pltpu.roll(value[at + 64 : at + 128], 64, 1))
            turned[2 * slot + part] = both.astype(BF16)

    def body(i, carry):
        for u in range(3):
            slot = 1 + 3 * i + u
            keep(slot, one(slot, slot))
        return carry

    keep(0, one(0, 0) + one(N_CTX, 0))
    lax.fori_loop(0, 21, body, 0)


def last_pass(turned, outer_inv, out):
    def body(jb, carry):
        rows = pl.ds(pl.multiple_of(jb * 16, 16), 16)
        t = turned[:, rows, :].astype(F32)
        t = jnp.concatenate(
            [t[:, 8 * h : 8 * h + 8].reshape(2 * SLOTS * 8, 128).astype(BF16) for h in range(2)], axis=1
        )
        y = jnp.dot(outer_inv[...], t, preferred_element_type=F32)
        y = jnp.concatenate([y[:, 128 * h : 128 * h + 128].reshape(N_CTX, 8, 128) for h in range(2)], axis=1)
        out[:, rows, :] = y.astype(BF16)
        return carry

    lax.fori_loop(0, 4, body, 0)


def kernel(
    grad_next, gate, conv_input, saved_conv, long_filter, outer_fwd_h, outer_inv_h, twist_h, turn_h,
    grad_input, grad_gate, filter_grad,
    v_in, v_fi, v_gate, v_saved, v_grad, v_gg, v_gc, outer_fwd, outer_inv, twist, turn,
    tx_both, tx_grad, rx_both, rx_grad, firsts, turned, tx_out, rx_out, v_gi, v_fg,
    load_sem, table_sem, store_sem, perm_sem, send_sem, recv_sem,
):
    me = lax.axis_index("ctx")
    section = lax.axis_index("section")
    x, y, z = me // 32, (me // 8) % 4, me % 8

    def peer(i):
        px, py, pz = (x + i // 32) % 2, (y + (i // 8) % 4) % 4, (z + i % 8) % 8
        return px * 32 + py * 8 + pz

    loads = [
        pltpu.make_async_copy(src, dst, load_sem.at[i])
        for i, (src, dst) in enumerate(
            [(conv_input, v_in), (long_filter, v_fi), (gate, v_gate), (saved_conv, v_saved)]
        )
    ]
    for load in loads:
        load.start()
    table_loads = [
        pltpu.make_async_copy(src, dst, table_sem.at[i])
        for i, (src, dst) in enumerate(
            [(outer_fwd_h, outer_fwd), (twist_h, twist), (turn_h, turn), (outer_inv_h, outer_inv)]
        )
    ]

    barrier = pltpu.get_barrier_semaphore()

    def greet(i, carry):
        pl.semaphore_signal(barrier, inc=1, device_id={"ctx": peer(i)}, device_id_type=MESH)
        return carry

    pl.semaphore_signal(barrier, inc=1, device_id={"section": (section + 1) % 4}, device_id_type=MESH)
    lax.fori_loop(1, N_CTX, greet, 0)

    loads[0].wait()
    loads[1].wait()
    pack_signal(v_in, tx_both.at[0], 0, 0)
    pack_signal(v_fi, tx_both.at[0], 0, 32)
    pl.semaphore_wait(barrier, N_CTX)

    passed = pltpu.make_async_remote_copy(
        src_ref=grad_next, dst_ref=v_grad, send_sem=perm_sem.at[0], recv_sem=perm_sem.at[1],
        device_id={"section": (section + 3) % 4}, device_id_type=MESH,
    )
    passed.start()

    def send(tx, rx, which):
        pltpu.make_async_copy(tx.at[me], rx.at[me], recv_sem.at[which]).start()

        def body(i, carry):
            d = peer(i)
            pltpu.make_async_remote_copy(
                src_ref=tx.at[d], dst_ref=rx.at[me], send_sem=send_sem.at[which], recv_sem=recv_sem.at[which],
                device_id={"ctx": d}, device_id_type=MESH,
            ).start()
            return carry

        lax.fori_loop(1, N_CTX, body, 0)

    def arrived(rx, which):
        pltpu.make_async_copy(rx, rx, recv_sem.at[which]).wait()

    def sent(tx, which):
        part = tx.at[pl.ds(0, N_CTX - 1)]
        pltpu.make_async_copy(part, part, send_sem.at[which]).wait()

    send(tx_both.at[0], rx_both.at[0], 0)
    for load in table_loads:
        load.start()
    pack_signal(v_in, tx_both.at[1], 1, 0)
    pack_signal(v_fi, tx_both.at[1], 1, 32)
    loads[2].wait()
    loads[3].wait()
    passed.wait_recv()

    def gating(r, carry):
        rows = pl.ds(pl.multiple_of(r * 16, 16), 16)
        grad = v_grad[rows, :].astype(F32)
        v_gc[rows, :] = (grad * v_gate[rows, :].astype(F32)).astype(BF16)
        v_gg[rows, :] = (grad * v_saved[rows, :].astype(F32)).astype(BF16)
        return carry

    lax.fori_loop(0, BLOCK // 16, gating, 0)
    pack_signal(v_gc, tx_grad.at[0], 0, 0)
    send(tx_grad.at[0], rx_grad.at[0], 1)
    send(tx_both.at[1], rx_both.at[1], 2)
    pack_signal(v_gc, tx_grad.at[1], 1, 0)
    send(tx_grad.at[1], rx_grad.at[1], 3)
    stores = [pltpu.make_async_copy(v_gg, grad_gate, store_sem.at[0])]
    stores[0].start()
    for load in table_loads:
        load.wait()

    for half in range(2):
        arrived(rx_both.at[half], 2 * half)
        arrived(rx_grad.at[half], 2 * half + 1)
        first_pass(rx_both.at[half], rx_grad.at[half], outer_fwd, firsts)
        middle_passes(firsts, twist, turn, turned)
        last_pass(turned, outer_inv, tx_out.at[half])
        send(tx_out.at[half], rx_out.at[half], 4 + half)

    for half in range(2):
        arrived(rx_out.at[half], 4 + half)
        unpack_outputs(rx_out.at[half], v_fg, v_gi, half)
        cols = pl.ds(half * HALF, HALF)
        for i, (src, dst) in enumerate([(v_gi, grad_input), (v_fg, filter_grad)]):
            store = pltpu.make_async_copy(src.at[:, cols], dst.at[:, cols], store_sem.at[1 + 2 * half + i])
            store.start()
            stores.append(store)

    passed.wait_send()
    for half in range(2):
        sent(tx_both.at[half], 2 * half)
        sent(tx_grad.at[half], 2 * half + 1)
        sent(tx_out.at[half], 4 + half)
    for store in stores:
        store.wait()


def per_device(consts, grad_next, gate, conv_input, saved_conv, long_filter):
    args = [a[0] for a in (grad_next, gate, conv_input, saved_conv, long_filter)]
    shard = jax.ShapeDtypeStruct((BLOCK, CHANNELS), BF16)
    any_spec = pl.BlockSpec(memory_space=pl.ANY)
    vmem = lambda *shape: pltpu.VMEM(shape, BF16)
    outs = pl.pallas_call(
        kernel,
        out_shape=[shard] * 3,
        in_specs=[any_spec] * 9,
        out_specs=[any_spec] * 3,
        scratch_shapes=[vmem(BLOCK, CHANNELS)] * 7
        + [vmem(*c.shape) for c in consts]
        + [
            vmem(2, N_CTX, 64, 128), vmem(2, N_CTX, 32, 128),
            vmem(2, N_CTX, 64, 128), vmem(2, N_CTX, 32, 128),
            vmem(2 * SLOTS, BLOCK, 128), vmem(2 * SLOTS, 64, 128),
            vmem(2, N_CTX, 64, 128), vmem(2, N_CTX, 64, 128),
            vmem(BLOCK, CHANNELS), vmem(BLOCK, CHANNELS),
            pltpu.SemaphoreType.DMA((4,)), pltpu.SemaphoreType.DMA((4,)), pltpu.SemaphoreType.DMA((5,)),
            pltpu.SemaphoreType.DMA((2,)), pltpu.SemaphoreType.DMA((6,)), pltpu.SemaphoreType.DMA((6,)),
        ],
        compiler_params=pltpu.CompilerParams(
            collective_id=0, has_side_effects=True, vmem_limit_bytes=58 * 2**20
        ),
    )(*args, *consts)
    return tuple(o[None] for o in outs)


def solution(mesh):
    consts = tables()
    spec = P("section", "ctx", None)
    return jax.shard_map(
        functools.partial(per_device, [jnp.asarray(c) for c in consts]),
        mesh=mesh, in_specs=(spec,) * 5, out_specs=(spec,) * 3, check_vma=False,
    )
```

time: 738 us -> 143 us (0.19); the launches traced: 728 us -> 141 us
  waiting for transfers between devices: 399 us -> 0 us
  local copies, waits for them, and re-layouts: 178 us -> 6.86 us
  Pallas kernels: 0 us -> 134 us
  starting transfers between devices: 82 us -> 0 us
  other arithmetic: 37.1 us -> 0 us
  matrix products: 30.2 us -> 0 us
    all_to_all x10 -> x0, waiting for transfers between devices: 399 us -> none  [the longest x3 184 us: spectrum_split(): lax.all_to_all(firsts, 'ctx', split_axis=0, concat_axis=2, tiled=True)]
    pallas_call x0 -> x1, Pallas kernels: none -> 134 us  [per_device(): pl.pallas_call(kernel, out_shape=[shard] * 3, in_specs=[any_spec] * 9, ou...]
    all_to_all x13 -> x0, local copies, waits for them, and re-layouts: 94.9 us -> none  [the longest x6 51.6 us: spectrum_split(): lax.all_to_all(firsts, 'ctx', split_axis=0, concat_axis=2, tiled=True)]
    all_to_all x10 -> x0, starting transfers between devices: 80.7 us -> none  [the longest x3 26.8 us: spectrum_split(): lax.all_to_all(firsts, 'ctx', split_axis=0, concat_axis=2, tiled=True)]
    unnamed x19 -> x3, local copies, waits for them, and re-layouts: 39 us -> 6.86 us
    dot_general x10 -> x0, matrix products: 30.2 us -> none  [the longest x3 14.8 us: second_pass(): jnp.einsum('koqij,kijw->koqw', matrix, row_data, preferred_element_type=j...]
    reshape x6 -> x0, local copies, waits for them, and re-layouts: 25.8 us -> none  [the longest x3 23.4 us: first_pass(): mixed_out.astype(jnp.bfloat16).reshape(outer_len, 2, local_rows, channels)]
    unnamed x3 -> x0, other arithmetic: 23.1 us -> none
  transfers between devices with their start and end apart: 11 -> 0, of which waited for: 10 -> 0; matrix products, arithmetic and copies ran while one was open for 26% -> 0% of each run, Pallas kernels for 0% -> 0%
where the time goes in v1:
time: 143 us; the launch traced here: 141 us
  Pallas kernels  134 us (94%)
  local copies, waits for them, and re-layouts  6.86 us (5%)
    pallas_call x1, Pallas kernels, per_device(): pl.pallas_call(kernel, out_shape=[shard] * 3, in_specs=[any_spec] * 9, ou...  134 us
    unnamed x3, local copies, waits for them, and re-layouts  6.86 us

profile of v1, /device:TPU:2, one launch (start us, length us, event | category | flops | bytes accessed | tf_op | source)
XLA Modules:
  0.0 141.3 jit_solution(17186024352629720995)
XLA Ops:
  0.6 133.8 %shard_map.112 = (bf16[128,4096]{1,0:T(8,128)(2,1)}, bf16[128,4096]{1,0:T(8,128)(2,1)}, bf16[128,4096]{1,0:T(8,128)(2,1)}) custom-call(bf16[128,4096]{1,0:T(8,128)(2,1)} %bitcast.8, bf16[128,4096]{1,0:T(8,128)(2,1)} %bitcast.9, bf16[128,4096]{1,0:T(8,128)(2,1)} %bitcast.10, bf16[128,4096]{1,0:T(8,128)(2,1)} %bitcast.11, bf16[128,4096]{1,0:T(8,128)(2,1)} %bitcast.12, ...), custom_call_target="tpu_custom_call" | custom-call | tf_op jit(solution)/shard_map/pallas_call | solution.py:300
  134.5 2.3 %copy.15 = bf16[1,128,4096]{2,1,0:T(8,128)(2,1)} copy(bf16[1,128,4096]{2,1,0:T(8,128)(2,1)} %bitcast.15) | data formatting | bytes 2097152
  136.7 2.3 %copy.16 = bf16[1,128,4096]{2,1,0:T(8,128)(2,1)} copy(bf16[1,128,4096]{2,1,0:T(8,128)(2,1)} %bitcast.14) | data formatting | bytes 2097152
  139.0 2.3 %copy.17 = bf16[1,128,4096]{2,1,0:T(8,128)(2,1)} copy(bf16[1,128,4096]{2,1,0:T(8,128)(2,1)} %bitcast.13) | data formatting | bytes 2097152

commit v2 on v1

--- a/solution.py
+++ b/solution.py
@@ -71,29 +71,28 @@
 
     def body(e, carry):
         cols = pl.ds(pl.multiple_of(half * HALF + e * 128, 128), 128)
-        quarters = [src[32 * q : 32 * q + 32, cols].astype(F32) for q in range(4)]
+        quarters = [src[32 * q : 32 * q + 32, cols] for q in range(4)]
         for g in range(4):
             parts = [rolled(quarters[q], 32 * (q - g)) for q in range(4)]
-            dst[4 * e + g, row : row + 32, :] = pick(groups, parts).astype(BF16)
+            dst[4 * e + g, row : row + 32, :] = pick(groups, parts)
         return carry
 
     lax.fori_loop(0, 16, body, 0)
 
 
-def unpack_outputs(src, filter_out, input_out, half):
+def unpack_outputs(src, filter_out, input_out, first, last):
     groups = lane_group((64, 128))
 
     def body(e, carry):
-        cols = pl.ds(pl.multiple_of(half * HALF + e * 128, 128), 128)
-        got = [src[4 * e + g].astype(F32) for g in range(4)]
+        cols = pl.ds(pl.multiple_of(e * 128, 128), 128)
+        got = [src[4 * e + g] for g in range(4)]
         for at in range(4):
             parts = [rolled(got[g], 32 * (g - at)) for g in range(4)]
-            value = pick(groups, parts).astype(BF16)
             out = (filter_out, input_out)[at % 2]
-            out[64 * (at // 2) : 64 * (at // 2) + 64, cols] = value
-        return carry
-
-    lax.fori_loop(0, 16, body, 0)
+            out[64 * (at // 2) : 64 * (at // 2) + 64, cols] = pick(groups, parts)
+        return carry
+
+    lax.fori_loop(first, last, body, 0)
 
 
 def first_pass(both, grad, outer_fwd, firsts):
@@ -127,14 +126,18 @@
 def middle_passes(firsts, twist, turn, turned):
     low = lax.broadcasted_iota(jnp.int32, (64, 128), 1) < 64
 
-    def one(k1, slot):
+    def spectra(k1, slot):
         data = firsts[pl.ds(2 * slot, 2)].reshape(2 * BLOCK, 128)
-        spec = jnp.dot(twist[k1], data, preferred_element_type=F32)
+        return jnp.dot(twist[k1], data, preferred_element_type=F32)
+
+    def crossed(spec):
         re, im = spec[:BLOCK], spec[BLOCK:]
         grad_re, grad_im = pltpu.roll(re, 64, 1), pltpu.roll(im, 64, 1)
-        cross = jnp.concatenate(
+        return jnp.concatenate(
             [(grad_re * re + grad_im * im).astype(BF16), (grad_im * re - grad_re * im).astype(BF16)], axis=0
         )
+
+    def turn_of(k1, cross):
         return jnp.dot(turn[k1], cross, preferred_element_type=F32)
 
     def keep(slot, value):
@@ -144,13 +147,16 @@
             turned[2 * slot + part] = both.astype(BF16)
 
     def body(i, carry):
-        for u in range(3):
-            slot = 1 + 3 * i + u
-            keep(slot, one(slot, slot))
-        return carry
-
-    keep(0, one(0, 0) + one(N_CTX, 0))
-    lax.fori_loop(0, 21, body, 0)
+        slots = [1 + 7 * i + u for u in range(7)]
+        specs = [spectra(k, k) for k in slots]
+        cross = [crossed(v) for v in specs]
+        turns = [turn_of(k, c) for k, c in zip(slots, cross)]
+        for k, t in zip(slots, turns):
+            keep(k, t)
+        return carry
+
+    keep(0, turn_of(0, crossed(spectra(0, 0))) + turn_of(N_CTX, crossed(spectra(N_CTX, 0))))
+    lax.fori_loop(0, 9, body, 0)
 
 
 def last_pass(turned, outer_inv, out):
@@ -170,9 +176,9 @@
 
 def kernel(
     grad_next, gate, conv_input, saved_conv, long_filter, outer_fwd_h, outer_inv_h, twist_h, turn_h,
-    grad_input, grad_gate, filter_grad,
+    gg_out, part_out, got,
     v_in, v_fi, v_gate, v_saved, v_grad, v_gg, v_gc, outer_fwd, outer_inv, twist, turn,
-    tx_both, tx_grad, rx_both, rx_grad, firsts, turned, tx_out, rx_out, v_gi, v_fg,
+    tx_both, tx_grad, rx_both, rx_grad, firsts, turned, tx_out, rx_out, v_part,
     load_sem, table_sem, store_sem, perm_sem, send_sem, recv_sem,
 ):
     me = lax.axis_index("ctx")
@@ -261,7 +267,7 @@
     send(tx_both.at[1], rx_both.at[1], 2)
     pack_signal(v_gc, tx_grad.at[1], 1, 0)
     send(tx_grad.at[1], rx_grad.at[1], 3)
-    stores = [pltpu.make_async_copy(v_gg, grad_gate, store_sem.at[0])]
+    stores = [pltpu.make_async_copy(v_gg, gg_out, store_sem.at[0])]
     stores[0].start()
     for load in table_loads:
         load.wait()
@@ -272,16 +278,13 @@
         first_pass(rx_both.at[half], rx_grad.at[half], outer_fwd, firsts)
         middle_passes(firsts, twist, turn, turned)
         last_pass(turned, outer_inv, tx_out.at[half])
-        send(tx_out.at[half], rx_out.at[half], 4 + half)
-
-    for half in range(2):
-        arrived(rx_out.at[half], 4 + half)
-        unpack_outputs(rx_out.at[half], v_fg, v_gi, half)
-        cols = pl.ds(half * HALF, HALF)
-        for i, (src, dst) in enumerate([(v_gi, grad_input), (v_fg, filter_grad)]):
-            store = pltpu.make_async_copy(src.at[:, cols], dst.at[:, cols], store_sem.at[1 + 2 * half + i])
-            store.start()
-            stores.append(store)
+        send(tx_out.at[half], (rx_out, got)[half], 4 + half)
+
+    arrived(rx_out, 4)
+    unpack_outputs(rx_out, v_part.at[0], v_part.at[1], 0, 16)
+    stores.append(pltpu.make_async_copy(v_part, part_out, store_sem.at[1]))
+    stores[1].start()
+    arrived(got, 5)
 
     passed.wait_send()
     for half in range(2):
@@ -292,6 +295,46 @@
         store.wait()
 
 
+def finish(
+    gg, part, got, grad_input, grad_gate, filter_grad, v_got, v_gg, v_fi, v_in, load_sem, gg_sem, part_sem, store_sem
+):
+    loads = [
+        pltpu.make_async_copy(got.at[pl.ds(16 * c, 16)], v_got.at[pl.ds(16 * c, 16)], load_sem.at[c]) for c in range(4)
+    ]
+    gg_loads = [
+        pltpu.make_async_copy(gg.at[pl.ds(64 * r, 64)], v_gg.at[pl.ds(64 * r, 64)], gg_sem.at[r]) for r in range(2)
+    ]
+    part_loads = [
+        pltpu.make_async_copy(part.at[i], v.at[:, pl.ds(0, HALF)], part_sem.at[i]) for i, v in enumerate((v_fi, v_in))
+    ]
+    for copy in loads + gg_loads + part_loads:
+        copy.start()
+    stores = []
+
+    def store(src, out):
+        stores.append(pltpu.make_async_copy(src, out, store_sem.at[len(stores)]))
+        stores[-1].start()
+
+    for c in range(4):
+        loads[c].wait()
+        unpack_outputs(
+            v_got.at[pl.ds(16 * c, 16)], v_fi.at[:, pl.ds(HALF + 512 * c, 512)],
+            v_in.at[:, pl.ds(HALF + 512 * c, 512)], 0, 4,
+        )
+        for src, out in ((v_fi, filter_grad), (v_in, grad_input)):
+            cols = pl.ds(HALF + 512 * c, 512)
+            store(src.at[:, cols], out.at[:, cols])
+        if c < 2:
+            gg_loads[c].wait()
+            store(v_gg.at[pl.ds(64 * c, 64)], grad_gate.at[pl.ds(64 * c, 64)])
+        else:
+            part_loads[c - 2].wait()
+            src, out = ((v_fi, filter_grad), (v_in, grad_input))[c - 2]
+            store(src.at[:, pl.ds(0, HALF)], out.at[:, pl.ds(0, HALF)])
+    for copy in stores:
+        copy.wait()
+
+
 def per_device(consts, grad_next, gate, conv_input, saved_conv, long_filter):
     args = [a[0] for a in (grad_next, gate, conv_input, saved_conv, long_filter)]
     shard = jax.ShapeDtypeStruct((BLOCK, CHANNELS), BF16)
@@ -299,7 +342,9 @@
     vmem = lambda *shape: pltpu.VMEM(shape, BF16)
     outs = pl.pallas_call(
         kernel,
-        out_shape=[shard] * 3,
+        out_shape=[
+            shard, jax.ShapeDtypeStruct((2, BLOCK, HALF), BF16), jax.ShapeDtypeStruct((N_CTX, 64, 128), BF16)
+        ],
         in_specs=[any_spec] * 9,
         out_specs=[any_spec] * 3,
         scratch_shapes=[vmem(BLOCK, CHANNELS)] * 7
@@ -308,15 +353,25 @@
             vmem(2, N_CTX, 64, 128), vmem(2, N_CTX, 32, 128),
             vmem(2, N_CTX, 64, 128), vmem(2, N_CTX, 32, 128),
             vmem(2 * SLOTS, BLOCK, 128), vmem(2 * SLOTS, 64, 128),
-            vmem(2, N_CTX, 64, 128), vmem(2, N_CTX, 64, 128),
-            vmem(BLOCK, CHANNELS), vmem(BLOCK, CHANNELS),
-            pltpu.SemaphoreType.DMA((4,)), pltpu.SemaphoreType.DMA((4,)), pltpu.SemaphoreType.DMA((5,)),
+            vmem(2, N_CTX, 64, 128), vmem(N_CTX, 64, 128), vmem(2, BLOCK, HALF),
+            pltpu.SemaphoreType.DMA((4,)), pltpu.SemaphoreType.DMA((4,)), pltpu.SemaphoreType.DMA((2,)),
             pltpu.SemaphoreType.DMA((2,)), pltpu.SemaphoreType.DMA((6,)), pltpu.SemaphoreType.DMA((6,)),
         ],
         compiler_params=pltpu.CompilerParams(
             collective_id=0, has_side_effects=True, vmem_limit_bytes=58 * 2**20
         ),
     )(*args, *consts)
+    outs = pl.pallas_call(
+        finish,
+        out_shape=[shard] * 3,
+        in_specs=[any_spec] * 3,
+        out_specs=[any_spec] * 3,
+        scratch_shapes=[
+            vmem(N_CTX, 64, 128), vmem(BLOCK, CHANNELS), vmem(BLOCK, CHANNELS), vmem(BLOCK, CHANNELS),
+            pltpu.SemaphoreType.DMA((4,)), pltpu.SemaphoreType.DMA((2,)),
+            pltpu.SemaphoreType.DMA((2,)), pltpu.SemaphoreType.DMA((12,)),
+        ],
+    )(*outs)
     return tuple(o[None] for o in outs)
 
 

time: 143 us -> 132 us (0.923)
  local copies, waits for them, and re-layouts: 6.86 us -> 0 us
  Pallas kernels: 134 us -> 130 us
    unnamed x3 -> x0, local copies, waits for them, and re-layouts: 6.86 us -> none
    pallas_call x1 -> x2, Pallas kernels: 134 us -> 130 us  [the longest x1 126 us: per_device(): pl.pallas_call(kernel, out_shape=[shard, jax.ShapeDtypeStruct((2, BLOCK,...]
where the time goes in v2:
time: 132 us; the launch traced here: 131 us
  Pallas kernels  130 us (98%)
    pallas_call x1, Pallas kernels, per_device(): pl.pallas_call(kernel, out_shape=[shard, jax.ShapeDtypeStruct((2, BLOCK,...  126 us
    pallas_call x1, Pallas kernels, per_device(): pl.pallas_call(finish, out_shape=[shard] * 3, in_specs=[any_spec] * 3, ou...  3.97 us

profile of v2, /device:TPU:2, one launch (start us, length us, event | category | flops | bytes accessed | tf_op | source)
XLA Modules:
  0.0 130.5 jit_solution(10584539641071631674)
XLA Ops:
  0.6 125.9 %shard_map.112 = (bf16[128,4096]{1,0:T(8,128)(2,1)}, bf16[2,128,2048]{2,1,0:T(8,128)(2,1)}, bf16[64,64,128]{2,1,0:T(8,128)(2,1)}) custom-call(bf16[128,4096]{1,0:T(8,128)(2,1)} %bitcast.8, bf16[128,4096]{1,0:T(8,128)(2,1)} %bitcast.9, bf16[128,4096]{1,0:T(8,128)(2,1)} %bitcast.10, bf16[128,4096]{1,0:T(8,128)(2,1)} %bitcast.11, bf16[128,4096]{1,0:T(8,128)(2,1)} %bitcast.12, ...), custom_call_target="tpu_custom_call" | custom-call | tf_op jit(solution)/shard_map/pallas_call | solution.py:343
  126.6 4.0 %shard_map.113 = (bf16[128,4096]{1,0:T(8,128)(2,1)}, bf16[128,4096]{1,0:T(8,128)(2,1)}, bf16[128,4096]{1,0:T(8,128)(2,1)}) custom-call(bf16[128,4096]{1,0:T(8,128)(2,1)} %get-tuple-element.9.gg, bf16[2,128,2048]{2,1,0:T(8,128)(2,1)} %get-tuple-element.10.part, bf16[64,64,128]{2,1,0:T(8,128)(2,1)} %get-tuple-element.11.got), custom_call_target="tpu_custom_call" | custom-call | tf_op jit(solution)/shard_map/pallas_call | solution.py:364

commit v3 on v2

--- a/solution.py
+++ b/solution.py
@@ -77,7 +77,7 @@
             dst[4 * e + g, row : row + 32, :] = pick(groups, parts)
         return carry
 
-    lax.fori_loop(0, 16, body, 0)
+    lax.fori_loop(0, 16, body, 0, unroll=4)
 
 
 def unpack_outputs(src, filter_out, input_out, first, last):
@@ -92,7 +92,7 @@
             out[64 * (at // 2) : 64 * (at // 2) + 64, cols] = pick(groups, parts)
         return carry
 
-    lax.fori_loop(first, last, body, 0)
+    lax.fori_loop(first, last, body, 0, unroll=4)
 
 
 def first_pass(both, grad, outer_fwd, firsts):
@@ -176,10 +176,10 @@
 
 def kernel(
     grad_next, gate, conv_input, saved_conv, long_filter, outer_fwd_h, outer_inv_h, twist_h, turn_h,
-    gg_out, part_out, got,
-    v_in, v_fi, v_gate, v_saved, v_grad, v_gg, v_gc, outer_fwd, outer_inv, twist, turn,
-    tx_both, tx_grad, rx_both, rx_grad, firsts, turned, tx_out, rx_out, v_part,
-    load_sem, table_sem, store_sem, perm_sem, send_sem, recv_sem,
+    v_gg, v_part, got,
+    v_in, v_fi, v_gate, v_saved, v_grad, v_gc, outer_fwd, outer_inv, twist, turn,
+    tx_both, tx_grad, rx_both, rx_grad, firsts, turned, tx_out, rx_out,
+    load_sem, table_sem, perm_sem, send_sem, recv_sem,
 ):
     me = lax.axis_index("ctx")
     section = lax.axis_index("section")
@@ -219,13 +219,19 @@
     pack_signal(v_fi, tx_both.at[0], 0, 32)
     pl.semaphore_wait(barrier, N_CTX)
 
-    passed = pltpu.make_async_remote_copy(
-        src_ref=grad_next, dst_ref=v_grad, send_sem=perm_sem.at[0], recv_sem=perm_sem.at[1],
-        device_id={"section": (section + 3) % 4}, device_id_type=MESH,
-    )
-    passed.start()
-
-    def send(tx, rx, which):
+    def pass_along(piece):
+        half = piece // 8
+        at = (pl.ds(pl.multiple_of(piece % 8 * 16, 16), 16), pl.ds(pl.multiple_of(half * HALF, HALF), HALF))
+        pltpu.make_async_remote_copy(
+            src_ref=grad_next.at[at], dst_ref=v_grad.at[at], send_sem=perm_sem.at[half], recv_sem=perm_sem.at[2 + half],
+            device_id={"section": (section + 3) % 4}, device_id_type=MESH,
+        ).start()
+
+    def passed(half, which):
+        part = v_grad.at[:, pl.ds(half * HALF, HALF)]
+        pltpu.make_async_copy(part, part, perm_sem.at[which]).wait()
+
+    def send(tx, rx, which, beside=False):
         pltpu.make_async_copy(tx.at[me], rx.at[me], recv_sem.at[which]).start()
 
         def body(i, carry):
@@ -234,6 +240,12 @@
                 src_ref=tx.at[d], dst_ref=rx.at[me], send_sem=send_sem.at[which], recv_sem=recv_sem.at[which],
                 device_id={"ctx": d}, device_id_type=MESH,
             ).start()
+            if beside:
+
+                @pl.when(i % 4 == 1)
+                def _():
+                    pass_along(i // 4)
+
             return carry
 
         lax.fori_loop(1, N_CTX, body, 0)
@@ -245,30 +257,35 @@
         part = tx.at[pl.ds(0, N_CTX - 1)]
         pltpu.make_async_copy(part, part, send_sem.at[which]).wait()
 
-    send(tx_both.at[0], rx_both.at[0], 0)
+    send(tx_both.at[0], rx_both.at[0], 0, beside=True)
     for load in table_loads:
         load.start()
     pack_signal(v_in, tx_both.at[1], 1, 0)
     pack_signal(v_fi, tx_both.at[1], 1, 32)
     loads[2].wait()
     loads[3].wait()
-    passed.wait_recv()
-
-    def gating(r, carry):
-        rows = pl.ds(pl.multiple_of(r * 16, 16), 16)
-        grad = v_grad[rows, :].astype(F32)
-        v_gc[rows, :] = (grad * v_gate[rows, :].astype(F32)).astype(BF16)
-        v_gg[rows, :] = (grad * v_saved[rows, :].astype(F32)).astype(BF16)
-        return carry
-
-    lax.fori_loop(0, BLOCK // 16, gating, 0)
+
+    def gating(half):
+        cols = pl.ds(half * HALF, HALF)
+
+        def body(r, carry):
+            rows = pl.ds(pl.multiple_of(r * 16, 16), 16)
+            grad = v_grad[rows, cols].astype(F32)
+            v_gc[rows, cols] = (grad * v_gate[rows, cols].astype(F32)).astype(BF16)
+            v_gg[rows, cols] = (grad * v_saved[rows, cols].astype(F32)).astype(BF16)
+            return carry
+
+        lax.fori_loop(0, BLOCK // 16, body, 0)
+
+    passed(0, 2)
+    gating(0)
     pack_signal(v_gc, tx_grad.at[0], 0, 0)
     send(tx_grad.at[0], rx_grad.at[0], 1)
     send(tx_both.at[1], rx_both.at[1], 2)
+    passed(1, 3)
+    gating(1)
     pack_signal(v_gc, tx_grad.at[1], 1, 0)
     send(tx_grad.at[1], rx_grad.at[1], 3)
-    stores = [pltpu.make_async_copy(v_gg, gg_out, store_sem.at[0])]
-    stores[0].start()
     for load in table_loads:
         load.wait()
 
@@ -282,55 +299,31 @@
 
     arrived(rx_out, 4)
     unpack_outputs(rx_out, v_part.at[0], v_part.at[1], 0, 16)
-    stores.append(pltpu.make_async_copy(v_part, part_out, store_sem.at[1]))
-    stores[1].start()
     arrived(got, 5)
 
-    passed.wait_send()
+    passed(0, 0)
+    passed(1, 1)
     for half in range(2):
         sent(tx_both.at[half], 2 * half)
         sent(tx_grad.at[half], 2 * half + 1)
         sent(tx_out.at[half], 4 + half)
-    for store in stores:
-        store.wait()
-
-
-def finish(
-    gg, part, got, grad_input, grad_gate, filter_grad, v_got, v_gg, v_fi, v_in, load_sem, gg_sem, part_sem, store_sem
-):
-    loads = [
-        pltpu.make_async_copy(got.at[pl.ds(16 * c, 16)], v_got.at[pl.ds(16 * c, 16)], load_sem.at[c]) for c in range(4)
-    ]
-    gg_loads = [
-        pltpu.make_async_copy(gg.at[pl.ds(64 * r, 64)], v_gg.at[pl.ds(64 * r, 64)], gg_sem.at[r]) for r in range(2)
-    ]
-    part_loads = [
-        pltpu.make_async_copy(part.at[i], v.at[:, pl.ds(0, HALF)], part_sem.at[i]) for i, v in enumerate((v_fi, v_in))
-    ]
-    for copy in loads + gg_loads + part_loads:
-        copy.start()
+
+
+def finish(gg, part, got, grad_input, grad_gate, filter_grad, v_fi, v_in, store_sem):
     stores = []
 
     def store(src, out):
         stores.append(pltpu.make_async_copy(src, out, store_sem.at[len(stores)]))
         stores[-1].start()
 
+    store(gg, grad_gate)
+    for i, out in enumerate((filter_grad, grad_input)):
+        store(part.at[i], out.at[:, pl.ds(0, HALF)])
     for c in range(4):
-        loads[c].wait()
-        unpack_outputs(
-            v_got.at[pl.ds(16 * c, 16)], v_fi.at[:, pl.ds(HALF + 512 * c, 512)],
-            v_in.at[:, pl.ds(HALF + 512 * c, 512)], 0, 4,
-        )
+        cols = pl.ds(512 * c, 512)
+        unpack_outputs(got.at[pl.ds(16 * c, 16)], v_fi.at[:, cols], v_in.at[:, cols], 0, 4)
         for src, out in ((v_fi, filter_grad), (v_in, grad_input)):
-            cols = pl.ds(HALF + 512 * c, 512)
-            store(src.at[:, cols], out.at[:, cols])
-        if c < 2:
-            gg_loads[c].wait()
-            store(v_gg.at[pl.ds(64 * c, 64)], grad_gate.at[pl.ds(64 * c, 64)])
-        else:
-            part_loads[c - 2].wait()
-            src, out = ((v_fi, filter_grad), (v_in, grad_input))[c - 2]
-            store(src.at[:, pl.ds(0, HALF)], out.at[:, pl.ds(0, HALF)])
+            store(src.at[:, cols], out.at[:, pl.ds(HALF + 512 * c, 512)])
     for copy in stores:
         copy.wait()
 
@@ -339,38 +332,34 @@
     args = [a[0] for a in (grad_next, gate, conv_input, saved_conv, long_filter)]
     shard = jax.ShapeDtypeStruct((BLOCK, CHANNELS), BF16)
     any_spec = pl.BlockSpec(memory_space=pl.ANY)
+    vmem_spec = pl.BlockSpec(memory_space=pltpu.VMEM)
     vmem = lambda *shape: pltpu.VMEM(shape, BF16)
     outs = pl.pallas_call(
         kernel,
-        out_shape=[
-            shard, jax.ShapeDtypeStruct((2, BLOCK, HALF), BF16), jax.ShapeDtypeStruct((N_CTX, 64, 128), BF16)
-        ],
+        out_shape=[vmem(BLOCK, CHANNELS), vmem(2, BLOCK, HALF), vmem(N_CTX, 64, 128)],
         in_specs=[any_spec] * 9,
-        out_specs=[any_spec] * 3,
-        scratch_shapes=[vmem(BLOCK, CHANNELS)] * 7
+        out_specs=[vmem_spec] * 3,
+        scratch_shapes=[vmem(BLOCK, CHANNELS)] * 6
         + [vmem(*c.shape) for c in consts]
         + [
             vmem(2, N_CTX, 64, 128), vmem(2, N_CTX, 32, 128),
             vmem(2, N_CTX, 64, 128), vmem(2, N_CTX, 32, 128),
             vmem(2 * SLOTS, BLOCK, 128), vmem(2 * SLOTS, 64, 128),
-            vmem(2, N_CTX, 64, 128), vmem(N_CTX, 64, 128), vmem(2, BLOCK, HALF),
-            pltpu.SemaphoreType.DMA((4,)), pltpu.SemaphoreType.DMA((4,)), pltpu.SemaphoreType.DMA((2,)),
-            pltpu.SemaphoreType.DMA((2,)), pltpu.SemaphoreType.DMA((6,)), pltpu.SemaphoreType.DMA((6,)),
+            vmem(2, N_CTX, 64, 128), vmem(N_CTX, 64, 128),
+            pltpu.SemaphoreType.DMA((4,)), pltpu.SemaphoreType.DMA((4,)),
+            pltpu.SemaphoreType.DMA((4,)), pltpu.SemaphoreType.DMA((6,)), pltpu.SemaphoreType.DMA((6,)),
         ],
         compiler_params=pltpu.CompilerParams(
-            collective_id=0, has_side_effects=True, vmem_limit_bytes=58 * 2**20
+            collective_id=0, has_side_effects=True, vmem_limit_bytes=50 * 2**20
         ),
     )(*args, *consts)
     outs = pl.pallas_call(
         finish,
         out_shape=[shard] * 3,
-        in_specs=[any_spec] * 3,
+        in_specs=[vmem_spec] * 3,
         out_specs=[any_spec] * 3,
-        scratch_shapes=[
-            vmem(N_CTX, 64, 128), vmem(BLOCK, CHANNELS), vmem(BLOCK, CHANNELS), vmem(BLOCK, CHANNELS),
-            pltpu.SemaphoreType.DMA((4,)), pltpu.SemaphoreType.DMA((2,)),
-            pltpu.SemaphoreType.DMA((2,)), pltpu.SemaphoreType.DMA((12,)),
-        ],
+        scratch_shapes=[vmem(BLOCK, HALF), vmem(BLOCK, HALF), pltpu.SemaphoreType.DMA((11,))],
+        compiler_params=pltpu.CompilerParams(vmem_limit_bytes=12 * 2**20),
     )(*outs)
     return tuple(o[None] for o in outs)
 

time: 132 us -> 129 us (0.977); the launches traced: 131 us -> 129 us
    pallas_call x2, Pallas kernels: 130 us -> 129 us  [the longest x1 127 us: per_device(): pl.pallas_call(kernel, out_shape=[vmem(BLOCK, CHANNELS), vmem(2, BLOCK, H...]
where the time goes in v3:
time: 129 us
  Pallas kernels  129 us (100%)
    pallas_call x1, Pallas kernels, per_device(): pl.pallas_call(kernel, out_shape=[vmem(BLOCK, CHANNELS), vmem(2, BLOCK, H...  127 us

profile of v3, /device:TPU:2, one launch (start us, length us, event | category | flops | bytes accessed | tf_op | source)
XLA Modules:
  0.0 129.2 jit_solution(3357743851630934238)
XLA Ops:
  0.6 126.8 %shard_map.112 = (bf16[128,4096]{1,0:T(8,128)(2,1)S(1)}, bf16[2,128,2048]{2,1,0:T(8,128)(2,1)S(1)}, bf16[64,64,128]{2,1,0:T(8,128)(2,1)S(1)}) custom-call(bf16[128,4096]{1,0:T(8,128)(2,1)} %bitcast.8, bf16[128,4096]{1,0:T(8,128)(2,1)} %bitcast.9, bf16[128,4096]{1,0:T(8,128)(2,1)} %bitcast.10, bf16[128,4096]{1,0:T(8,128)(2,1)} %bitcast.11, ...), custom_call_target="tpu_custom_call" | custom-call | tf_op jit(solution)/shard_map/pallas_call | solution.py:337
  127.4 1.8 %shard_map.113 = (bf16[128,4096]{1,0:T(8,128)(2,1)}, bf16[128,4096]{1,0:T(8,128)(2,1)}, bf16[128,4096]{1,0:T(8,128)(2,1)}) custom-call(bf16[128,4096]{1,0:T(8,128)(2,1)S(1)} %get-tuple-element.9.gg, bf16[2,128,2048]{2,1,0:T(8,128)(2,1)S(1)} %get-tuple-element.10.part, bf16[64,64,128]{2,1,0:T(8,128)(2,1)S(1)} %get-tuple-element.11.got), custom_call_target="tpu_custom_call" | custom-call | tf_op jit(solution)/shard_map/pallas_call | solution.py:356

commit v4 on v3

--- a/solution.py
+++ b/solution.py
@@ -189,13 +189,18 @@
         px, py, pz = (x + i // 32) % 2, (y + (i // 8) % 4) % 4, (z + i % 8) % 8
         return px * 32 + py * 8 + pz
 
+    first, second = pl.ds(0, HALF), pl.ds(HALF, HALF)
     loads = [
         pltpu.make_async_copy(src, dst, load_sem.at[i])
         for i, (src, dst) in enumerate(
-            [(conv_input, v_in), (long_filter, v_fi), (gate, v_gate), (saved_conv, v_saved)]
+            [
+                (conv_input.at[:, first], v_in.at[:, first]), (long_filter.at[:, first], v_fi.at[:, first]),
+                (conv_input.at[:, second], v_in.at[:, second]), (long_filter.at[:, second], v_fi.at[:, second]),
+                (gate, v_gate), (saved_conv, v_saved),
+            ]
         )
     ]
-    for load in loads:
+    for load in loads[:2]:
         load.start()
     table_loads = [
         pltpu.make_async_copy(src, dst, table_sem.at[i])
@@ -214,8 +219,10 @@
     lax.fori_loop(1, N_CTX, greet, 0)
 
     loads[0].wait()
+    pack_signal(v_in, tx_both.at[0], 0, 0)
     loads[1].wait()
-    pack_signal(v_in, tx_both.at[0], 0, 0)
+    for load in loads[2:]:
+        load.start()
     pack_signal(v_fi, tx_both.at[0], 0, 32)
     pl.semaphore_wait(barrier, N_CTX)
 
@@ -260,10 +267,10 @@
     send(tx_both.at[0], rx_both.at[0], 0, beside=True)
     for load in table_loads:
         load.start()
+    for load in loads[2:]:
+        load.wait()
     pack_signal(v_in, tx_both.at[1], 1, 0)
     pack_signal(v_fi, tx_both.at[1], 1, 32)
-    loads[2].wait()
-    loads[3].wait()
 
     def gating(half):
         cols = pl.ds(half * HALF, HALF)
@@ -346,7 +353,7 @@
             vmem(2, N_CTX, 64, 128), vmem(2, N_CTX, 32, 128),
             vmem(2 * SLOTS, BLOCK, 128), vmem(2 * SLOTS, 64, 128),
             vmem(2, N_CTX, 64, 128), vmem(N_CTX, 64, 128),
-            pltpu.SemaphoreType.DMA((4,)), pltpu.SemaphoreType.DMA((4,)),
+            pltpu.SemaphoreType.DMA((6,)), pltpu.SemaphoreType.DMA((4,)),
             pltpu.SemaphoreType.DMA((4,)), pltpu.SemaphoreType.DMA((6,)), pltpu.SemaphoreType.DMA((6,)),
         ],
         compiler_params=pltpu.CompilerParams(

time: 129 us -> 129 us (level)
  no operation moved by 1% of the time
where the time goes in v4:
time: 129 us
  Pallas kernels  129 us (100%)
    pallas_call x1, Pallas kernels, per_device(): pl.pallas_call(kernel, out_shape=[vmem(BLOCK, CHANNELS), vmem(2, BLOCK, H...  127 us

profile of v4, /device:TPU:2, one launch (start us, length us, event | category | flops | bytes accessed | tf_op | source)
XLA Modules:
  0.0 129.2 jit_solution(16923676007192259807)
XLA Ops:
  0.6 126.8 %shard_map.112 = (bf16[128,4096]{1,0:T(8,128)(2,1)S(1)}, bf16[2,128,2048]{2,1,0:T(8,128)(2,1)S(1)}, bf16[64,64,128]{2,1,0:T(8,128)(2,1)S(1)}) custom-call(bf16[128,4096]{1,0:T(8,128)(2,1)} %bitcast.8, bf16[128,4096]{1,0:T(8,128)(2,1)} %bitcast.9, bf16[128,4096]{1,0:T(8,128)(2,1)} %bitcast.10, bf16[128,4096]{1,0:T(8,128)(2,1)} %bitcast.11, ...), custom_call_target="tpu_custom_call" | custom-call | tf_op jit(solution)/shard_map/pallas_call | solution.py:344
  127.4 1.8 %shard_map.113 = (bf16[128,4096]{1,0:T(8,128)(2,1)}, bf16[128,4096]{1,0:T(8,128)(2,1)}, bf16[128,4096]{1,0:T(8,128)(2,1)}) custom-call(bf16[128,4096]{1,0:T(8,128)(2,1)S(1)} %get-tuple-element.9.gg, bf16[2,128,2048]{2,1,0:T(8,128)(2,1)S(1)} %get-tuple-element.10.part, bf16[64,64,128]{2,1,0:T(8,128)(2,1)S(1)} %get-tuple-element.11.got), custom_call_target="tpu_custom_call" | custom-call | tf_op jit(solution)/shard_map/pallas_call | solution.py:363
